TPU v7x, 256 devices: a whole 4x4x8 slice. The times are simulated.
256 devices in a mesh: str: 64 (over y, z, core), ib: 4 (over x).
Axes of the slice: x: 4, y: 4, z: 8, core: 2. Of those that a mesh axis runs over, the one named last changes fastest.
Arguments:
- coeffs: bfloat16 [256, 32768], P('str'), may hold values from -6 to 6
- block_irrep: int32 [256], replicated, may hold values from 0 to 7
- couple_block: int32 [256, 8], replicated, may hold values from 0 to 255
- couple_sign: int32 [256, 8], replicated, may hold values from -1 to 1
- block_order: int32 [256], replicated, may hold values from 0 to 255, each once
- alpha_same: bfloat16 [256, 256], replicated, may hold values from -0.375 to 0.375
- alpha_mixed: bfloat16 [8, 256, 256], P('ib'), may hold values from -0.125 to 0.125
- beta_same: bfloat16 [8, 128, 128], replicated, may hold values from -0.1875 to 0.1875
- beta_mixed: bfloat16 [8, 8, 128, 128], P('ib'), may hold values from -0.1875 to 0.1875
Outputs:
- sigma: bfloat16 [256, 32768], P(None, ('str', 'ib'))
Inputs may be any that keep to these rules, and one draw needn't show every extreme that they name: `block_order`: a permutation of the block numbers.
All inputs are finite; a program needn't handle non-finite values.
Results may differ from a plain program's by a relative error of at most 0.0047.
Values may be sent and summed in bfloat16 or wider, within the bound.
A program may use at most 64 MiB of HBM per device.

v0:
```python
import jax
import jax.numpy as jnp
from jax import lax
from jax.sharding import PartitionSpec as P


def group_rows(blocks, block_irrep, couple_block, couple_sign, chosen):
    alpha_rows = blocks.shape[0]
    block_size = blocks.shape[2]
    coupled = couple_block[chosen]
    sign_rows = couple_sign[chosen]
    kind_rows = jnp.bitwise_xor(block_irrep[chosen][:, None], block_irrep[coupled])
    weights = jnp.where(
        kind_rows[:, :, None] == jnp.arange(8, dtype=jnp.int32)[None, None, :],
        sign_rows[:, :, None],
        0,
    ).astype(jnp.bfloat16)
    picked = blocks[:, coupled]
    grouped = jnp.einsum(
        "ajkc,jkq->ajqc", picked, weights, preferred_element_type=jnp.float32
    ).astype(jnp.bfloat16)
    return grouped.reshape(alpha_rows * chosen.shape[0], 8 * block_size)


def local(
    coeffs,
    block_irrep,
    couple_block,
    couple_sign,
    block_order,
    alpha_same,
    alpha_mixed,
    beta_same,
    beta_mixed,
):
    alpha_rows = coeffs.shape[0]
    block_count = couple_block.shape[0]
    block_size = beta_same.shape[1]
    str_count = lax.axis_size("str")
    ib_count = lax.axis_size("ib")
    per_device = block_count // str_count
    per_quarter = per_device // ib_count
    alpha_total = alpha_same.shape[0]
    blocks = coeffs.reshape(alpha_rows, block_count, block_size)
    quarter = per_quarter * block_size
    ib_place = lax.axis_index("ib")
    offset = ib_place * quarter
    pair_count = alpha_mixed.shape[0]
    grouped = group_rows(blocks, block_irrep, couple_block, couple_sign, block_order)
    mix_weights = jnp.transpose(beta_mixed, (1, 2, 0, 3)).reshape(
        8 * block_size, pair_count * block_size
    )
    mixed_beta = jnp.dot(grouped, mix_weights, preferred_element_type=jnp.float32).astype(
        jnp.bfloat16
    )
    mixed_send = mixed_beta.reshape(alpha_rows, str_count, per_device * pair_count * block_size)
    same_beta = jnp.dot(
        grouped, beta_same.reshape(8 * block_size, block_size), preferred_element_type=jnp.float32
    ).astype(jnp.bfloat16)
    owned_cols = blocks[:, block_order].reshape(alpha_rows, str_count, per_device * block_size)
    same_send = same_beta.reshape(alpha_rows, str_count, per_device * block_size)
    mixed_recv, cols_recv, same_recv = (
        lax.all_to_all(mixed_send, "str", split_axis=1, concat_axis=0, tiled=True),
        lax.all_to_all(owned_cols, "str", split_axis=1, concat_axis=0, tiled=True),
        lax.all_to_all(same_send, "str", split_axis=1, concat_axis=0, tiled=True),
    )
    cols_mine = lax.dynamic_slice_in_dim(
        cols_recv.reshape(alpha_total, per_device * block_size), offset, quarter, 1
    )
    same_mine = lax.dynamic_slice_in_dim(
        same_recv.reshape(alpha_total, per_device * block_size), offset, quarter, 1
    )
    mixed_grid = mixed_recv.reshape(alpha_total, per_device, pair_count, block_size)
    partial_value = jnp.einsum(
        "pab,bjpd->ajd", alpha_mixed, mixed_grid, preferred_element_type=jnp.float32
    )
    partial_value = partial_value.reshape(alpha_total, per_device * block_size)
    summed = lax.psum_scatter(partial_value, "ib", scatter_dimension=1, tiled=True)
    same_term = jnp.dot(
        alpha_same, cols_mine, preferred_element_type=jnp.float32
    ) + same_mine.astype(jnp.float32)
    return (summed + same_term).astype(jnp.bfloat16)


def solution(mesh):
    in_specs = (
        P("str", None),
        P(),
        P(),
        P(),
        P(),
        P(),
        P("ib", None, None),
        P(),
        P("ib", None, None, None),
    )
    out_specs = P(None, ("str", "ib"))
    return jax.shard_map(local, mesh=mesh, in_specs=in_specs, out_specs=out_specs, check_vma=False)
```

profile of v0, /device:TPU:4, one launch (start us, length us, event | category | flops | bytes accessed | tf_op | source)
XLA Modules:
  0.0 116.9 jit_solution(15202733848219670929)
XLA Ops:
  6.5 0.0 copy-start
  6.5 0.0 copy-start.1
  6.5 0.0 reduce-scatter.2.cloned.1.call-start
  6.5 0.7 compare_select_fusion.1
  7.3 0.8 copy.15
  8.1 0.7 gather_fusion.1
  8.9 0.1 reshape.97
  9.0 0.0 copy-done.1
  9.0 1.9 %gather_fusion = s32[256]{0:T(256)S(1)} fusion(s32[256]{0:T(256)S(1)} %copy-done.1, s32[1024]{0:T(1024)S(1)} %pad_clamp_fusion), kind=kCustom, calls=%fused_computation | custom fusion | bytes 3072 | tf_op jit(solution)/shard_map/gather | solution.py:12
  11.0 13.2 %gather_fusion.2 = s32[2048]{0:T(1024)S(1)} fusion(s32[256]{0:T(256)S(1)} %copy-done.1, s32[2048]{0:T(1024)S(1)} %broadcast_clamp_fusion), kind=kCustom, calls=%fused_computation.2 | custom fusion | bytes 24576 | tf_op jit(solution)/shard_map/gather | solution.py:12
  24.2 0.1 reshape.96
  24.3 0.0 copy-done
  24.3 0.0 copy-start.4
  24.3 6.9 %gather_fusion.4 = bf16[2048,4,128]{2,1,0:T(4,128)(2,1)S(1)} fusion(bf16[4,256,128]{2,0,1:T(4,128)(2,1)S(1)} %bitcast.75, s32[2048]{0:T(1024)S(1)} %broadcast_clamp_fusion), kind=kCustom, calls=%fused_computation.4 | custom fusion | bytes 4202496 | tf_op jit(solution)/shard_map/gather | solution.py:18
  31.2 0.0 copy-done.4
  31.2 0.1 copy.16
  31.3 0.7 gather_fusion.3
  32.0 0.1 broadcast_xor_fusion
  32.1 0.7 convert_bitcast_fusion
  32.8 0.0 copy-start.2
  32.8 0.4 copy.19
  33.2 0.7 copy-done.2
  33.9 1.1 copy.20
  35.0 1.8 %fusion.10 = bf16[1024,256]{1,0:T(8,128)(2,1)S(1)} fusion(bf16[128,8,8,128]{3,2,1,0:T(8,128)(2,1)S(1)} %bitcast.77, bf16[32,8,8,128]{3,2,1,0:T(8,128)(2,1)} %bitcast.84), kind=kOutput, calls=%fused_computation.16 | convolution fusion | flops 537133056 | bytes 3145728 | tf_op jit(solution)/shard_map/dot_general | solution.py:53
  36.8 0.3 reshape.71
  37.1 0.4 copy.21
  37.5 29.1 %all_to_all.45 = bf16[4,64,1024]{2,0,1:T(4,128)(2,1)S(1)} all-to-all(bf16[4,64,1024]{2,0,1:T(4,128)(2,1)S(1)} %copy.21), channel_id=1, replica_groups=mesh['str'=64,'ib'=4] {'str'}, dimensions={1} | all-to-all | bytes 1048576 | tf_op jit(solution)/shard_map/all_to_all | solution.py:63
  66.6 0.2 reshape.72
  66.8 2.1 %fusion.23 = f32[4,128,256,1]{2,1,3,0:T(8,128)} fusion(bf16[256,4,2,128]{3,2,1,0:T(2,128)(2,1)S(1)} %reshape.72, bf16[2,256,256]{2,1,0:T(8,128)(2,1)} %param.15), kind=kOutput, calls=%fused_computation.27 | convolution fusion | flops 134217728 | bytes 1310720 | tf_op jit(solution)/shard_map/pab,bjpd->ajd/dot_general | solution.py:74
  68.9 0.0 reduce-scatter.2.cloned.1.call-update
  68.9 1.7 %fusion.13 = bf16[1024,128]{1,0:T(8,128)(2,1)S(1)} fusion(bf16[1024,128]{1,0:T(8,128)(2,1)} %bitcast.85, bf16[128,8,8,128]{3,2,1,0:T(8,128)(2,1)S(1)} %bitcast.78), kind=kOutput, calls=%fused_computation.17 | convolution fusion | flops 268566528 | bytes 2621440 | tf_op jit(solution)/shard_map/dot_general | solution.py:57
  70.6 0.0 copy-start.3
  70.6 0.2 reshape.77
  70.8 0.9 copy.23
  71.7 6.4 %all-to-all-start.2 = ((bf16[4,64,512]{2,0,1:T(4,128)(2,1)}), bf16[4,64,512]{2,0,1:T(4,128)(2,1)S(1)}, u32[]{:S(2)}, u32[]{:S(2)}) async-start(bf16[4,64,512]{2,0,1:T(4,128)(2,1)} %copy.23), calls=%async_computation.3 | async-start | bytes 524288 | tf_op jit(solution)/shard_map/all_to_all | solution.py:65
  78.1 1.7 %gather_fusion.5 = bf16[256,4,128]{2,1,0:T(4,128)(2,1)} fusion(bf16[4,256,128]{2,0,1:T(4,128)(2,1)S(1)} %bitcast.76, s32[1024]{0:T(1024)S(1)} %pad_clamp_fusion), kind=kCustom, calls=%fused_computation.5 | custom fusion | bytes 525312 | tf_op jit(solution)/shard_map/gather | solution.py:60
  79.8 10.3 %all-to-all-done.2 = bf16[4,64,512]{2,0,1:T(4,128)(2,1)S(1)} async-done(((bf16[4,64,512]{2,0,1:T(4,128)(2,1)}), bf16[4,64,512]{2,0,1:T(4,128)(2,1)S(1)}, u32[]{:S(2)}, u32[]{:S(2)}) %all-to-all-start.2) | async-done | bytes 262176 | tf_op jit(solution)/shard_map/all_to_all | solution.py:65
  90.1 6.0 %all-to-all-start.1 = ((bf16[4,64,512]{2,0,1:T(4,128)(2,1)}), bf16[4,64,512]{2,0,1:T(4,128)(2,1)S(1)}, u32[]{:S(2)}, u32[]{:S(2)}) async-start(bf16[4,64,512]{2,0,1:T(4,128)(2,1)} %bitcast.16), calls=%async_computation.2 | async-start | bytes 524288 | tf_op jit(solution)/shard_map/all_to_all | solution.py:64
  96.1 0.1 reshape.78
  96.2 0.1 copy.28
  96.4 11.8 %all-to-all-done.1 = bf16[4,64,512]{2,0,1:T(4,128)(2,1)S(1)} async-done(((bf16[4,64,512]{2,0,1:T(4,128)(2,1)}), bf16[4,64,512]{2,0,1:T(4,128)(2,1)S(1)}, u32[]{:S(2)}, u32[]{:S(2)}) %all-to-all-start.1) | async-done | bytes 262176 | tf_op jit(solution)/shard_map/all_to_all | solution.py:64
  108.1 0.1 reshape.75
  108.2 0.0 reduce-scatter.2.cloned.1.call-done
  108.2 0.0 copy-done.3
  108.2 1.1 fusion.18
  109.4 0.7 copy.25
  (4 shorter events, 0.0 us)
Async XLA Ops:
  6.5 17.7 %copy-start = (bf16[4,32768]{1,0:T(4,128)(2,1)S(1)}, bf16[4,32768]{1,0:T(4,128)(2,1)}, u32[]{:S(2)}) copy-start(bf16[4,32768]{1,0:T(4,128)(2,1)} %param.9) | copy-start | bytes 786436
  6.5 2.5 %copy-start.1 = (s32[256]{0:T(256)S(1)}, s32[256]{0:T(256)}, u32[]{:S(2)}) copy-start(s32[256]{0:T(256)} %param.10) | copy-start | bytes 3076
  6.5 101.7 %reduce-scatter.2.cloned.1.call-start = ((), (), s32[]{:S(2)}) async-start(), calls=%async_computation.4 | async-start | bytes 655360 | tf_op jit(solution)/shard_map/reduce_scatter | solution.py:78
  24.3 6.9 %copy-start.4 = (s32[256,8]{0,1:T(8,128)S(1)}, s32[256,8]{0,1:T(8,128)}, u32[]{:S(2)}) copy-start(s32[256,8]{0,1:T(8,128)} %param.12) | copy-start | bytes 24580
  32.8 1.0 copy-start.2
  70.6 37.6 %copy-start.3 = (bf16[256,256]{1,0:T(8,128)(2,1)S(1)}, bf16[256,256]{1,0:T(8,128)(2,1)}, u32[]{:S(2)}) copy-start(bf16[256,256]{1,0:T(8,128)(2,1)} %param.14) | copy-start | bytes 393220
  71.7 18.4 %all-to-all-start.2 = ((bf16[4,64,512]{2,0,1:T(4,128)(2,1)}), bf16[4,64,512]{2,0,1:T(4,128)(2,1)S(1)}, u32[]{:S(2)}, u32[]{:S(2)}) async-start(bf16[4,64,512]{2,0,1:T(4,128)(2,1)} %copy.23), calls=%async_computation.3 | async-start | bytes 524288 | tf_op jit(solution)/shard_map/all_to_all | solution.py:65
  90.1 18.0 %all-to-all-start.1 = ((bf16[4,64,512]{2,0,1:T(4,128)(2,1)}), bf16[4,64,512]{2,0,1:T(4,128)(2,1)S(1)}, u32[]{:S(2)}, u32[]{:S(2)}) async-start(bf16[4,64,512]{2,0,1:T(4,128)(2,1)} %bitcast.16), calls=%async_computation.2 | async-start | bytes 524288 | tf_op jit(solution)/shard_map/all_to_all | solution.py:64
Sparse Core Ops, SparseCore 0:
  69.0 19.5 reduce-scatter.1
where the time goes:
time: 118 us; the launch traced here: 117 us
  local copies, waits for them, and re-layouts  31.4 us (27%)
  blocking collectives  29.1 us (25%)
  waiting for transfers between devices  22.2 us (19%)
  between operations  13.6 us (12%)
  starting transfers between devices  12.4 us (11%)
  matrix products  7.35 us (6%)
    all_to_all x1, blocking collectives, local(): lax.all_to_all(mixed_send, 'str', split_axis=1, concat_axis=0, tiled=True)  29.1 us
    gather x2, local copies, waits for them, and re-layouts, group_rows(): block_irrep[coupled]  13.3 us
    all_to_all x1, waiting for transfers between devices, local(): lax.all_to_all(owned_cols, 'str', split_axis=1, concat_axis=0, tiled=True)  11.8 us
    all_to_all x1, waiting for transfers between devices, local(): lax.all_to_all(same_send, 'str', split_axis=1, concat_axis=0, tiled=True)  10.3 us
    gather x1, local copies, waits for them, and re-layouts, group_rows(): picked = blocks[:, coupled]  6.86 us
    all_to_all x1, starting transfers between devices, local(): lax.all_to_all(same_send, 'str', split_axis=1, concat_axis=0, tiled=True)  6.41 us
    all_to_all x1, starting transfers between devices, local(): lax.all_to_all(owned_cols, 'str', split_axis=1, concat_axis=0, tiled=True)  6.03 us
  transfers between devices with their start and end apart: 3, of which 2 were waited for; matrix products, arithmetic and copies ran while one was open for 4% of the time, Pallas kernels for 0%

commit v1 on v0

v1 whole, which is shorter than its diff:
```python
import functools

import jax
import jax.numpy as jnp
from jax import lax
from jax.experimental import pallas as pl
from jax.experimental.pallas import tpu as pltpu
from jax.sharding import PartitionSpec as P

MESH = pl.DeviceIdType.MESH
F32 = jnp.float32
BF16 = jnp.bfloat16


def iota(shape, dim):
    return lax.broadcasted_iota(jnp.int32, shape, dim)


def kernel(
    n_str,
    n_ib,
    coef_ref,
    irr_ref,
    cb_ref,
    sg_ref,
    ord_ref,
    as_hbm,
    am_hbm,
    bs_hbm,
    bm_hbm,
    out_ref,
    b_ref,
    a_ref,
    as_ref,
    g_ref,
    z_ref,
    send_a,
    send_b,
    recv_a,
    recv_b,
    part_s,
    part_r,
    load_sem,
    str_send,
    str_recv,
    ib_send,
    ib_recv,
):
    me = lax.axis_index("str")
    ib = lax.axis_index("ib")

    barrier = pltpu.get_barrier_semaphore()

    def greet(k, carry):
        pl.semaphore_signal(
            barrier, inc=1, device_id=(lax.rem(me + k, n_str), ib), device_id_type=MESH
        )
        return carry

    lax.fori_loop(1, n_str, greet, 0)
    for k in range(1, n_ib):
        pl.semaphore_signal(
            barrier, inc=1, device_id=(me, lax.rem(ib + k, n_ib)), device_id_type=MESH
        )

    loads = [
        pltpu.make_async_copy(bm_hbm.at[0], b_ref.at[:, pl.ds(0, 128)], load_sem.at[0]),
        pltpu.make_async_copy(bm_hbm.at[1], b_ref.at[:, pl.ds(128, 128)], load_sem.at[1]),
        pltpu.make_async_copy(bs_hbm, b_ref.at[:, pl.ds(256, 128)], load_sem.at[2]),
        pltpu.make_async_copy(am_hbm.at[0], a_ref.at[:, pl.ds(0, 256)], load_sem.at[3]),
        pltpu.make_async_copy(am_hbm.at[1], a_ref.at[:, pl.ds(256, 256)], load_sem.at[4]),
        pltpu.make_async_copy(as_hbm, as_ref, load_sem.at[5]),
    ]
    for load in loads:
        load.start()

    cb = cb_ref[...]
    sg = sg_ref[...]
    row = iota((256, 256), 0)
    counts = jnp.zeros((256, 256), jnp.int32)
    for k in range(8):
        counts = counts + jnp.where(row == cb[k : k + 1, :], sg[k : k + 1, :], 0)
    counts = counts.astype(F32).astype(BF16)
    irr = irr_ref[...]
    irr_f = irr.astype(F32)
    order_f = ord_ref[...].astype(F32)
    lane = iota((64, 256), 1)
    sub = iota((64, 256), 0)
    lane_f = lane.astype(F32)
    coef = coef_ref[...]

    r = iota((512, 512), 0)
    c = iota((512, 512), 1)
    to_msg = jnp.where(
        c == (r // 4 % 2) * 256 + (r % 4) * 64 + r // 8, 1.0, 0.0
    ).astype(BF16)

    def unit(t, slot, last):
        place = lax.rem(ib + t, n_ib)
        owned = jnp.sum(
            jnp.where(lane == 4 * sub + place, order_f, 0.0), axis=1, keepdims=True
        )
        pick = lane_f == owned
        irr_row = jnp.sum(jnp.where(pick, irr_f, 0.0), axis=1, keepdims=True).astype(jnp.int32)
        pick = jnp.where(pick, 1.0, 0.0).astype(BF16)
        near = lax.dot_general(
            pick, counts, (((1,), (1,)), ((), ())), preferred_element_type=F32
        )
        kind = jnp.bitwise_xor(irr_row, irr)
        weights = jnp.concatenate(
            [jnp.where(kind == q, near, 0.0) for q in range(8)], axis=0
        ).astype(BF16)
        grouped = jnp.dot(weights, coef, preferred_element_type=F32).astype(BF16)
        for q in range(8):
            for a in range(4):
                g_ref[a * 64 : (a + 1) * 64, q * 128 : (q + 1) * 128] = grouped[
                    q * 64 : (q + 1) * 64, a * 128 : (a + 1) * 128
                ]
        at = pl.ds(slot * 128, 128)
        cols = 384 if last else 256
        mixed = jnp.dot(g_ref[...], b_ref[:, :cols], preferred_element_type=F32).astype(BF16)
        z_ref[0:256, at] = mixed[:, 0:128]
        z_ref[256:512, at] = mixed[:, 128:256]
        if last:
            at = pl.ds(slot * 128 + 128, 128)
            own = jnp.dot(pick, coef, preferred_element_type=F32).astype(BF16)
            for a in range(4):
                z_ref[a * 64 : (a + 1) * 64, at] = own[:, a * 128 : (a + 1) * 128]
            z_ref[256:512, at] = mixed[:, 256:384]

    def pack(lo, width):
        rows = jnp.dot(to_msg, z_ref[:, lo : lo + width], preferred_element_type=F32)
        return rows.reshape(64, 8, width).astype(BF16)

    def send_all(src, dst, which):
        def one(k, carry):
            to = lax.rem(me + k, n_str)
            pltpu.make_async_remote_copy(
                src_ref=src.at[to],
                dst_ref=dst.at[me],
                send_sem=str_send.at[which],
                recv_sem=str_recv.at[which],
                device_id=(to, ib),
                device_id_type=MESH,
            ).start()
            return carry

        lax.fori_loop(1, n_str, one, 0)

    def await_all(ref, sem):
        some = ref.at[pl.ds(0, n_str - 1)]
        pltpu.make_async_copy(some, some, sem).wait()

    for load in loads[:3]:
        load.wait()
    for t in range(1, 4):
        unit(t, t - 1, False)
    send_a[...] = pack(0, 384)
    pl.semaphore_wait(barrier, n_str - 1 + n_ib - 1)
    send_all(send_a, recv_a, 0)
    unit(0, 3, True)
    send_b[...] = pack(384, 256)
    send_all(send_b, recv_b, 1)

    recv_a[me] = send_a[me]
    recv_b[me] = send_b[me]
    from_cols = jnp.where(
        r == (c // 4 % 2) * 256 + (c // 8) * 4 + c % 4, 1.0, 0.0
    ).astype(BF16)
    for load in loads[3:]:
        load.wait()
    alpha = jnp.dot(a_ref[...], from_cols, preferred_element_type=F32).astype(BF16)
    eye = jnp.where(iota((256, 256), 0) == iota((256, 256), 1), 1.0, 0.0).astype(BF16)
    same = jnp.concatenate([as_ref[...], eye], axis=1)
    same = jnp.dot(same, from_cols, preferred_element_type=F32).astype(BF16)

    def received(ref):
        x = ref[...].astype(F32)
        return x.reshape(512, x.shape[2]).astype(BF16)

    await_all(recv_a, str_recv.at[0])
    partial = jnp.dot(alpha, received(recv_a), preferred_element_type=F32).astype(BF16)
    copies = []
    for u in range(3):
        part_s[u] = partial[:, u * 128 : (u + 1) * 128]
        copy = pltpu.make_async_remote_copy(
            src_ref=part_s.at[u],
            dst_ref=part_r.at[u],
            send_sem=ib_send.at[u],
            recv_sem=ib_recv.at[u],
            device_id=(me, lax.rem(ib + 1 + u, n_ib)),
            device_id_type=MESH,
        )
        copy.start()
        copies.append(copy)
    await_all(recv_b, str_recv.at[1])
    x = received(recv_b)
    total = jnp.dot(alpha, x[:, 0:128], preferred_element_type=F32) + jnp.dot(
        same, x[:, 128:256], preferred_element_type=F32
    )
    for u in range(3):
        copies[u].wait_recv()
        total = total + part_r[u].astype(F32)
    out_ref[...] = total.astype(BF16)
    for u in range(3):
        copies[u].wait_send()
    await_all(send_a, str_send.at[0])
    await_all(send_b, str_send.at[1])


def local(
    n_str,
    n_ib,
    coeffs,
    block_irrep,
    couple_block,
    couple_sign,
    block_order,
    alpha_same,
    alpha_mixed,
    beta_same,
    beta_mixed,
):
    coef = coeffs.reshape(4, 256, 128).transpose(1, 0, 2).reshape(256, 512)
    vmem = pl.BlockSpec(memory_space=pltpu.VMEM)
    any_ = pl.BlockSpec(memory_space=pl.ANY)
    return pl.pallas_call(
        functools.partial(kernel, n_str, n_ib),
        out_shape=jax.ShapeDtypeStruct((256, 128), BF16),
        in_specs=[vmem] * 5 + [any_] * 4,
        out_specs=vmem,
        scratch_shapes=[
            pltpu.VMEM((1024, 384), BF16),
            pltpu.VMEM((256, 512), BF16),
            pltpu.VMEM((256, 256), BF16),
            pltpu.VMEM((256, 1024), BF16),
            pltpu.VMEM((512, 640), BF16),
            pltpu.VMEM((64, 8, 384), BF16),
            pltpu.VMEM((64, 8, 256), BF16),
            pltpu.VMEM((64, 8, 384), BF16),
            pltpu.VMEM((64, 8, 256), BF16),
            pltpu.VMEM((3, 256, 128), BF16),
            pltpu.VMEM((3, 256, 128), BF16),
            pltpu.SemaphoreType.DMA((6,)),
            pltpu.SemaphoreType.DMA((2,)),
            pltpu.SemaphoreType.DMA((2,)),
            pltpu.SemaphoreType.DMA((3,)),
            pltpu.SemaphoreType.DMA((3,)),
        ],
        compiler_params=pltpu.CompilerParams(
            collective_id=0, has_side_effects=True, vmem_limit_bytes=48 * 1024 * 1024
        ),
    )(
        coef,
        block_irrep.reshape(1, 256),
        couple_block.T,
        couple_sign.T,
        block_order.reshape(1, 256),
        alpha_same,
        alpha_mixed,
        beta_same.reshape(1024, 128),
        beta_mixed.reshape(2, 1024, 128),
    )


def solution(mesh):
    in_specs = (
        P("str", None),
        P(),
        P(),
        P(),
        P(),
        P(),
        P("ib", None, None),
        P(),
        P("ib", None, None, None),
    )
    body = functools.partial(local, mesh.shape["str"], mesh.shape["ib"])
    return jax.shard_map(
        body, mesh=mesh, in_specs=in_specs, out_specs=P(None, ("str", "ib")), check_vma=False
    )
```

time: 118 us -> 35.4 us (0.30)
  the two profiles are of different devices: /device:TPU:4 before, /device:TPU:1 now
where the time goes in v1:
time: 35.4 us; the launch traced here: 35.2 us
  Pallas kernels  29.3 us (83%)
  local copies, waits for them, and re-layouts  5.87 us (17%)
    pallas_call x1, Pallas kernels, local(): pl.pallas_call(functools.partial(kernel, n_str, n_ib), out_shape=jax.Shap...  29.3 us
    unnamed x18, local copies, waits for them, and re-layouts  5.87 us

profile of v1, /device:TPU:1, one launch (start us, length us, event | category | flops | bytes accessed | tf_op | source)
XLA Modules:
  0.0 35.2 jit_solution(12568259282131922605)
XLA Ops:
  0.0 0.0 copy-start
  0.0 0.0 copy-start.4
  0.0 0.0 copy-start.7
  0.0 1.0 %copy.13 = bf16[32,8,4,128]{3,1,2,0:T(8,128)(2,1)S(1)} copy(bf16[32,8,4,128]{3,2,1,0:T(4,128)(2,1)} %bitcast.20) | data formatting | bytes 524288
  1.1 0.0 copy-start.6
  1.1 0.0 copy-done
  1.1 0.0 copy-done.4
  1.1 0.0 copy-done.7
  1.1 0.6 %copy-done.6 = s32[256]{0:T(256)S(1)} copy-done((s32[256]{0:T(256)S(1)}, s32[256]{0:T(256)}, u32[]{:S(2)}) %copy-start.6) | copy-done | bytes 1048
  1.8 0.0 copy-start.1
  1.8 0.9 %copy-done.1 = bf16[2,256,256]{2,1,0:T(8,128)(2,1)S(1)} copy-done((bf16[2,256,256]{2,1,0:T(8,128)(2,1)S(1)}, bf16[2,256,256]{2,1,0:T(8,128)(2,1)}, u32[]{:S(2)}) %copy-start.1) | copy-done | bytes 262168
  2.7 0.0 copy-start.2
  2.7 0.9 %copy-done.2 = bf16[8,128,128]{2,1,0:T(8,128)(2,1)S(1)} copy-done((bf16[8,128,128]{2,1,0:T(8,128)(2,1)S(1)}, bf16[8,128,128]{2,1,0:T(8,128)(2,1)}, u32[]{:S(2)}) %copy-start.2) | copy-done | bytes 262168
  3.7 0.0 copy-start.3
  3.7 0.9 %copy-done.3 = bf16[256,256]{1,0:T(8,128)(2,1)S(1)} copy-done((bf16[256,256]{1,0:T(8,128)(2,1)S(1)}, bf16[256,256]{1,0:T(8,128)(2,1)}, u32[]{:S(2)}) %copy-start.3) | copy-done | bytes 131096
  4.6 0.0 copy-start.5
  4.6 0.7 %copy-done.5 = s32[256,8]{0,1:T(8,128)S(1)} copy-done((s32[256,8]{0,1:T(8,128)S(1)}, s32[256,8]{0,1:T(8,128)}, u32[]{:S(2)}) %copy-start.5) | copy-done | bytes 8216
  5.3 29.3 %shard_map.91 = bf16[256,128]{1,0:T(8,128)(2,1)S(1)} custom-call(bf16[256,512]{1,0:T(8,128)(2,1)S(1)} %bitcast.13, s32[1,256]{1,0:T(1,128)S(1)} %bitcast.18, s32[8,256]{1,0:T(8,128)S(1)} %bitcast.16, s32[8,256]{1,0:T(8,128)S(1)} %bitcast.17, s32[1,256]{1,0:T(1,128)S(1)} %bitcast.19, bf16[256,256]{1,0:T(8,128)(2,1)S(1)} %copy-done.3, ...), custom_call_target="tpu_custom_call" | custom-call | tf_op jit(solution)/shard_map/pallas_call | solution.py:227
  34.6 0.6 %copy.15 = bf16[256,128]{1,0:T(8,128)(2,1)} copy(bf16[256,128]{1,0:T(8,128)(2,1)S(1)} %shard_map.91) | data formatting | bytes 131072
Async XLA Ops:
  0.0 1.1 %copy-start = (bf16[2,8,128,128]{3,2,1,0:T(8,128)(2,1)S(1)}, bf16[2,8,128,128]{3,2,1,0:T(8,128)(2,1)}, u32[]{:S(2)}) copy-start(bf16[2,8,128,128]{3,2,1,0:T(8,128)(2,1)} %param.17) | copy-start | bytes 1572868
  0.0 1.1 %copy-start.4 = (s32[256,8]{0,1:T(8,128)S(1)}, s32[256,8]{0,1:T(8,128)}, u32[]{:S(2)}) copy-start(s32[256,8]{0,1:T(8,128)} %param.11) | copy-start | bytes 24580
  0.0 1.1 %copy-start.7 = (s32[256]{0:T(256)S(1)}, s32[256]{0:T(256)}, u32[]{:S(2)}) copy-start(s32[256]{0:T(256)} %param.13) | copy-start | bytes 3076
  1.1 0.7 %copy-start.6 = (s32[256]{0:T(256)S(1)}, s32[256]{0:T(256)}, u32[]{:S(2)}) copy-start(s32[256]{0:T(256)} %param.10) | copy-start | bytes 3076
  1.8 0.9 %copy-start.1 = (bf16[2,256,256]{2,1,0:T(8,128)(2,1)S(1)}, bf16[2,256,256]{2,1,0:T(8,128)(2,1)}, u32[]{:S(2)}) copy-start(bf16[2,256,256]{2,1,0:T(8,128)(2,1)} %am_hbm.1) | copy-start | bytes 786436
  2.7 0.9 %copy-start.2 = (bf16[8,128,128]{2,1,0:T(8,128)(2,1)S(1)}, bf16[8,128,128]{2,1,0:T(8,128)(2,1)}, u32[]{:S(2)}) copy-start(bf16[8,128,128]{2,1,0:T(8,128)(2,1)} %param.16) | copy-start | bytes 786436
  3.7 0.9 %copy-start.3 = (bf16[256,256]{1,0:T(8,128)(2,1)S(1)}, bf16[256,256]{1,0:T(8,128)(2,1)}, u32[]{:S(2)}) copy-start(bf16[256,256]{1,0:T(8,128)(2,1)} %as_hbm.1) | copy-start | bytes 393220
  4.6 0.7 %copy-start.5 = (s32[256,8]{0,1:T(8,128)S(1)}, s32[256,8]{0,1:T(8,128)}, u32[]{:S(2)}) copy-start(s32[256,8]{0,1:T(8,128)} %param.12) | copy-start | bytes 24580

commit v2 on v1

--- a/solution.py
+++ b/solution.py
@@ -19,16 +19,23 @@
 def kernel(
     n_str,
     n_ib,
-    coef_ref,
-    irr_ref,
-    cb_ref,
-    sg_ref,
-    ord_ref,
+    coef_hbm,
+    irr_hbm,
+    cb_hbm,
+    sg_hbm,
+    ord_hbm,
     as_hbm,
     am_hbm,
     bs_hbm,
     bm_hbm,
     out_ref,
+    coef_ref,
+    coef_f,
+    c_ref,
+    irr_ref,
+    cb_ref,
+    sg_ref,
+    ord_ref,
     b_ref,
     a_ref,
     as_ref,
@@ -49,6 +56,22 @@
     me = lax.axis_index("str")
     ib = lax.axis_index("ib")
 
+    loads = [
+        pltpu.make_async_copy(cb_hbm, cb_ref, load_sem.at[0]),
+        pltpu.make_async_copy(sg_hbm, sg_ref, load_sem.at[1]),
+        pltpu.make_async_copy(irr_hbm, irr_ref, load_sem.at[2]),
+        pltpu.make_async_copy(ord_hbm, ord_ref, load_sem.at[3]),
+        pltpu.make_async_copy(coef_hbm, coef_ref, load_sem.at[4]),
+        pltpu.make_async_copy(bm_hbm.at[0], b_ref.at[:, pl.ds(0, 128)], load_sem.at[5]),
+        pltpu.make_async_copy(bm_hbm.at[1], b_ref.at[:, pl.ds(128, 128)], load_sem.at[6]),
+        pltpu.make_async_copy(bs_hbm, b_ref.at[:, pl.ds(256, 128)], load_sem.at[7]),
+        pltpu.make_async_copy(am_hbm.at[0], a_ref.at[:, pl.ds(0, 256)], load_sem.at[8]),
+        pltpu.make_async_copy(am_hbm.at[1], a_ref.at[:, pl.ds(256, 256)], load_sem.at[9]),
+        pltpu.make_async_copy(as_hbm, as_ref, load_sem.at[10]),
+    ]
+    for load in loads:
+        load.start()
+
     barrier = pltpu.get_barrier_semaphore()
 
     def greet(k, carry):
@@ -63,16 +86,13 @@
             barrier, inc=1, device_id=(me, lax.rem(ib + k, n_ib)), device_id_type=MESH
         )
 
-    loads = [
-        pltpu.make_async_copy(bm_hbm.at[0], b_ref.at[:, pl.ds(0, 128)], load_sem.at[0]),
-        pltpu.make_async_copy(bm_hbm.at[1], b_ref.at[:, pl.ds(128, 128)], load_sem.at[1]),
-        pltpu.make_async_copy(bs_hbm, b_ref.at[:, pl.ds(256, 128)], load_sem.at[2]),
-        pltpu.make_async_copy(am_hbm.at[0], a_ref.at[:, pl.ds(0, 256)], load_sem.at[3]),
-        pltpu.make_async_copy(am_hbm.at[1], a_ref.at[:, pl.ds(256, 256)], load_sem.at[4]),
-        pltpu.make_async_copy(as_hbm, as_ref, load_sem.at[5]),
-    ]
-    for load in loads:
-        load.start()
+    r = iota((512, 512), 0)
+    c = iota((512, 512), 1)
+    for load in loads[:8]:
+        load.wait()
+    coef_f[...] = coef_ref[...].astype(F32)
+    for a in range(4):
+        c_ref[:, a * 128 : (a + 1) * 128] = coef_f[:, a, :].astype(BF16)
 
     cb = cb_ref[...]
     sg = sg_ref[...]
@@ -87,10 +107,7 @@
     lane = iota((64, 256), 1)
     sub = iota((64, 256), 0)
     lane_f = lane.astype(F32)
-    coef = coef_ref[...]
-
-    r = iota((512, 512), 0)
-    c = iota((512, 512), 1)
+
     to_msg = jnp.where(
         c == (r // 4 % 2) * 256 + (r % 4) * 64 + r // 8, 1.0, 0.0
     ).astype(BF16)
@@ -110,7 +127,7 @@
         weights = jnp.concatenate(
             [jnp.where(kind == q, near, 0.0) for q in range(8)], axis=0
         ).astype(BF16)
-        grouped = jnp.dot(weights, coef, preferred_element_type=F32).astype(BF16)
+        grouped = jnp.dot(weights, c_ref[...], preferred_element_type=F32).astype(BF16)
         for q in range(8):
             for a in range(4):
                 g_ref[a * 64 : (a + 1) * 64, q * 128 : (q + 1) * 128] = grouped[
@@ -123,7 +140,7 @@
         z_ref[256:512, at] = mixed[:, 128:256]
         if last:
             at = pl.ds(slot * 128 + 128, 128)
-            own = jnp.dot(pick, coef, preferred_element_type=F32).astype(BF16)
+            own = jnp.dot(pick, c_ref[...], preferred_element_type=F32).astype(BF16)
             for a in range(4):
                 z_ref[a * 64 : (a + 1) * 64, at] = own[:, a * 128 : (a + 1) * 128]
             z_ref[256:512, at] = mixed[:, 256:384]
@@ -151,8 +168,6 @@
         some = ref.at[pl.ds(0, n_str - 1)]
         pltpu.make_async_copy(some, some, sem).wait()
 
-    for load in loads[:3]:
-        load.wait()
     for t in range(1, 4):
         unit(t, t - 1, False)
     send_a[...] = pack(0, 384)
@@ -162,13 +177,13 @@
     send_b[...] = pack(384, 256)
     send_all(send_b, recv_b, 1)
 
+    for load in loads[8:]:
+        load.wait()
     recv_a[me] = send_a[me]
     recv_b[me] = send_b[me]
     from_cols = jnp.where(
         r == (c // 4 % 2) * 256 + (c // 8) * 4 + c % 4, 1.0, 0.0
     ).astype(BF16)
-    for load in loads[3:]:
-        load.wait()
     alpha = jnp.dot(a_ref[...], from_cols, preferred_element_type=F32).astype(BF16)
     eye = jnp.where(iota((256, 256), 0) == iota((256, 256), 1), 1.0, 0.0).astype(BF16)
     same = jnp.concatenate([as_ref[...], eye], axis=1)
@@ -221,15 +236,20 @@
     beta_same,
     beta_mixed,
 ):
-    coef = coeffs.reshape(4, 256, 128).transpose(1, 0, 2).reshape(256, 512)
-    vmem = pl.BlockSpec(memory_space=pltpu.VMEM)
-    any_ = pl.BlockSpec(memory_space=pl.ANY)
+    hbm = pl.BlockSpec(memory_space=pltpu.HBM)
     return pl.pallas_call(
         functools.partial(kernel, n_str, n_ib),
         out_shape=jax.ShapeDtypeStruct((256, 128), BF16),
-        in_specs=[vmem] * 5 + [any_] * 4,
-        out_specs=vmem,
+        in_specs=[hbm] * 9,
+        out_specs=pl.BlockSpec(memory_space=pltpu.VMEM),
         scratch_shapes=[
+            pltpu.VMEM((256, 4, 128), BF16),
+            pltpu.VMEM((256, 4, 128), F32),
+            pltpu.VMEM((256, 512), BF16),
+            pltpu.VMEM((1, 256), jnp.int32),
+            pltpu.VMEM((8, 256), jnp.int32),
+            pltpu.VMEM((8, 256), jnp.int32),
+            pltpu.VMEM((1, 256), jnp.int32),
             pltpu.VMEM((1024, 384), BF16),
             pltpu.VMEM((256, 512), BF16),
             pltpu.VMEM((256, 256), BF16),
@@ -241,17 +261,17 @@
             pltpu.VMEM((64, 8, 256), BF16),
             pltpu.VMEM((3, 256, 128), BF16),
             pltpu.VMEM((3, 256, 128), BF16),
-            pltpu.SemaphoreType.DMA((6,)),
+            pltpu.SemaphoreType.DMA((11,)),
             pltpu.SemaphoreType.DMA((2,)),
             pltpu.SemaphoreType.DMA((2,)),
             pltpu.SemaphoreType.DMA((3,)),
             pltpu.SemaphoreType.DMA((3,)),
         ],
         compiler_params=pltpu.CompilerParams(
-            collective_id=0, has_side_effects=True, vmem_limit_bytes=48 * 1024 * 1024
+            collective_id=0, has_side_effects=True, vmem_limit_bytes=62 * 1024 * 1024
         ),
     )(
-        coef,
+        coeffs.reshape(4, 256, 128).transpose(1, 0, 2),
         block_irrep.reshape(1, 256),
         couple_block.T,
         couple_sign.T,

time: 35.4 us -> 31.8 us (0.90)
  local copies, waits for them, and re-layouts: 5.87 us -> 1.47 us
  Pallas kernels: 29.3 us -> 30.2 us
    unnamed x18 -> x1, local copies, waits for them, and re-layouts: 5.87 us -> 1.47 us
    pallas_call x1, Pallas kernels: 29.3 us -> 30.2 us  [local(): pl.pallas_call(functools.partial(kernel, n_str, n_ib), out_shape=jax.Shap...]
where the time goes in v2:
time: 31.8 us; the launch traced here: 31.7 us
  Pallas kernels  30.2 us (95%)
  local copies, waits for them, and re-layouts  1.47 us (5%)
    pallas_call x1, Pallas kernels, local(): pl.pallas_call(functools.partial(kernel, n_str, n_ib), out_shape=jax.Shap...  30.2 us
    unnamed x1, local copies, waits for them, and re-layouts  1.47 us

profile of v2, /device:TPU:1, one launch (start us, length us, event | category | flops | bytes accessed | tf_op | source)
XLA Modules:
  0.0 31.7 jit_solution(16933819719541258467)
XLA Ops:
  0.0 30.2 %shard_map.91 = bf16[256,128]{1,0:T(8,128)(2,1)} custom-call(bf16[256,4,128]{2,1,0:T(4,128)(2,1)} %bitcast.10, s32[1,256]{1,0:T(1,128)} %bitcast.14, s32[8,256]{1,0:T(8,128)} %bitcast.12, s32[8,256]{1,0:T(8,128)} %bitcast.13, s32[1,256]{1,0:T(1,128)} %bitcast.15, bf16[256,256]{1,0:T(8,128)(2,1)} %as_hbm.1, bf16[2,256,256]{2,1,0:T(8,128)(2,1)} %am_hbm.1, ...), custom_call_target="tpu_custom_call" | custom-call | tf_op jit(solution)/shard_map/pallas_call | solution.py:240
  30.2 1.5 %copy.11 = bf16[256,128]{1,0:T(8,128)(2,1)} copy(bf16[256,128]{1,0:T(8,128)(2,1)} %shard_map.91) | data formatting | bytes 131072

commit v3 on v2

--- a/solution.py
+++ b/solution.py
@@ -39,6 +39,7 @@
     b_ref,
     a_ref,
     as_ref,
+    msg_ref,
     g_ref,
     z_ref,
     send_a,
@@ -52,6 +53,9 @@
     str_recv,
     ib_send,
     ib_recv,
+    late_sem,
+    plane_sem,
+    all_sem,
 ):
     me = lax.axis_index("str")
     ib = lax.axis_index("ib")
@@ -72,31 +76,43 @@
     for load in loads:
         load.start()
 
+    y, z, core = me // 16, (me // 2) % 8, me % 2
+    late = z >= 4
+
+    def place(y_to, z_to, core_to):
+        return (((y_to % 4) * 8) + (z_to % 8)) * 2 + core_to % 2
+
     barrier = pltpu.get_barrier_semaphore()
 
-    def greet(k, carry):
+    def say(sem, y_to, z_to, core_to):
         pl.semaphore_signal(
-            barrier, inc=1, device_id=(lax.rem(me + k, n_str), ib), device_id_type=MESH
-        )
-        return carry
-
-    lax.fori_loop(1, n_str, greet, 0)
+            sem, inc=1, device_id=(place(y_to, z_to, core_to), ib), device_id_type=MESH
+        )
+
     for k in range(1, n_ib):
         pl.semaphore_signal(
             barrier, inc=1, device_id=(me, lax.rem(ib + k, n_ib)), device_id_type=MESH
         )
 
-    r = iota((512, 512), 0)
-    c = iota((512, 512), 1)
-    for load in loads[:8]:
+    for k in range(1, 64):
+        pl.semaphore_signal(
+            barrier, inc=1, device_id=((me + k) % 64, ib), device_id_type=MESH
+        )
+
+    r = iota((256, 256), 0)
+    c = iota((256, 256), 1)
+    msg_ref[...] = jnp.where(
+        c == (r // 4 % 2) * 128 + (r % 4) * 32 + r // 8, 1.0, 0.0
+    ).astype(BF16)
+    lane = iota((32, 256), 1)
+    sub = iota((32, 256), 0)
+    lane_f = lane.astype(F32)
+    row = iota((256, 256), 0)
+
+    for load in loads[:4]:
         load.wait()
-    coef_f[...] = coef_ref[...].astype(F32)
-    for a in range(4):
-        c_ref[:, a * 128 : (a + 1) * 128] = coef_f[:, a, :].astype(BF16)
-
     cb = cb_ref[...]
     sg = sg_ref[...]
-    row = iota((256, 256), 0)
     counts = jnp.zeros((256, 256), jnp.int32)
     for k in range(8):
         counts = counts + jnp.where(row == cb[k : k + 1, :], sg[k : k + 1, :], 0)
@@ -104,56 +120,75 @@
     irr = irr_ref[...]
     irr_f = irr.astype(F32)
     order_f = ord_ref[...].astype(F32)
-    lane = iota((64, 256), 1)
-    sub = iota((64, 256), 0)
-    lane_f = lane.astype(F32)
-
-    to_msg = jnp.where(
-        c == (r // 4 % 2) * 256 + (r % 4) * 64 + r // 8, 1.0, 0.0
-    ).astype(BF16)
-
-    def unit(t, slot, last):
-        place = lax.rem(ib + t, n_ib)
+
+    loads[4].wait()
+    coef_f[...] = coef_ref[...].astype(F32)
+    for a in range(4):
+        c_ref[:, a * 128 : (a + 1) * 128] = coef_f[:, a, :].astype(BF16)
+    for load in loads[5:8]:
+        load.wait()
+
+    def choose(t, half):
+        owner = (sub // 8) * 16 + (4 * half + sub // 2 % 4) * 2 + sub % 2
+        position = lax.rem(ib + t, n_ib)
         owned = jnp.sum(
-            jnp.where(lane == 4 * sub + place, order_f, 0.0), axis=1, keepdims=True
-        )
-        pick = lane_f == owned
-        irr_row = jnp.sum(jnp.where(pick, irr_f, 0.0), axis=1, keepdims=True).astype(jnp.int32)
-        pick = jnp.where(pick, 1.0, 0.0).astype(BF16)
+            jnp.where(lane == 4 * owner + position, order_f, 0.0), axis=1, keepdims=True
+        )
+        return jnp.where(lane_f == owned, 1.0, 0.0)
+
+    def units(ts, half, cols):
+        n = len(ts)
+        pick = jnp.concatenate([choose(t, half) for t in ts], axis=0)
+        irr_row = jnp.sum(pick * irr_f, axis=1, keepdims=True).astype(jnp.int32)
+        pick = pick.astype(BF16)
         near = lax.dot_general(
             pick, counts, (((1,), (1,)), ((), ())), preferred_element_type=F32
         )
         kind = jnp.bitwise_xor(irr_row, irr)
         weights = jnp.concatenate(
-            [jnp.where(kind == q, near, 0.0) for q in range(8)], axis=0
-        ).astype(BF16)
+            [jnp.where(kind == q, near, 0.0).astype(BF16) for q in range(8)], axis=0
+        )
         grouped = jnp.dot(weights, c_ref[...], preferred_element_type=F32).astype(BF16)
         for q in range(8):
-            for a in range(4):
-                g_ref[a * 64 : (a + 1) * 64, q * 128 : (q + 1) * 128] = grouped[
-                    q * 64 : (q + 1) * 64, a * 128 : (a + 1) * 128
-                ]
-        at = pl.ds(slot * 128, 128)
-        cols = 384 if last else 256
-        mixed = jnp.dot(g_ref[...], b_ref[:, :cols], preferred_element_type=F32).astype(BF16)
-        z_ref[0:256, at] = mixed[:, 0:128]
-        z_ref[256:512, at] = mixed[:, 128:256]
-        if last:
-            at = pl.ds(slot * 128 + 128, 128)
-            own = jnp.dot(pick, c_ref[...], preferred_element_type=F32).astype(BF16)
-            for a in range(4):
-                z_ref[a * 64 : (a + 1) * 64, at] = own[:, a * 128 : (a + 1) * 128]
-            z_ref[256:512, at] = mixed[:, 256:384]
-
-    def pack(lo, width):
-        rows = jnp.dot(to_msg, z_ref[:, lo : lo + width], preferred_element_type=F32)
-        return rows.reshape(64, 8, width).astype(BF16)
-
-    def send_all(src, dst, which):
+            for u in range(n):
+                for a in range(4):
+                    g_ref[u * 128 + a * 32 : u * 128 + (a + 1) * 32, q * 128 : (q + 1) * 128] = (
+                        grouped[q * n * 32 + u * 32 : q * n * 32 + (u + 1) * 32, a * 128 : (a + 1) * 128]
+                    )
+        mixed = jnp.dot(
+            g_ref[: n * 128, :], b_ref[:, :cols], preferred_element_type=F32
+        ).astype(BF16)
+        for u in range(n):
+            z_ref[0:128, u * 128 : (u + 1) * 128] = mixed[u * 128 : (u + 1) * 128, 0:128]
+            z_ref[128:256, u * 128 : (u + 1) * 128] = mixed[u * 128 : (u + 1) * 128, 128:256]
+        return pick, mixed
+
+    def pack(width):
+        rows = jnp.dot(msg_ref[...], z_ref[:, :width], preferred_element_type=F32)
+        return rows.reshape(32, 8, width).astype(BF16)
+
+    def chunk_a(half):
+        units((1, 2, 3), half, 256)
+        send_a[half * 32 : (half + 1) * 32] = pack(384)
+
+    def chunk_b(half):
+        pick, mixed = units((0,), half, 384)
+        own = jnp.dot(pick, c_ref[...], preferred_element_type=F32).astype(BF16)
+        for a in range(4):
+            z_ref[a * 32 : (a + 1) * 32, 128:256] = own[:, a * 128 : (a + 1) * 128]
+        z_ref[128:256, 128:256] = mixed[:, 256:384]
+        send_b[half * 32 : (half + 1) * 32] = pack(256)
+
+    sends = ((send_a, recv_a), (send_b, recv_b))
+
+    def send(which, z_to):
+        src, dst = sends[which]
+
         def one(k, carry):
-            to = lax.rem(me + k, n_str)
+            y_to, core_to = (y + k // 2) % 4, (core + k) % 2
+            to = place(y_to, z_to, core_to)
             pltpu.make_async_remote_copy(
-                src_ref=src.at[to],
+                src_ref=src.at[(z_to // 4) * 32 + y_to * 8 + (z_to % 4) * 2 + core_to],
                 dst_ref=dst.at[me],
                 send_sem=str_send.at[which],
                 recv_sem=str_recv.at[which],
@@ -162,28 +197,43 @@
             ).start()
             return carry
 
-        lax.fori_loop(1, n_str, one, 0)
+        lax.fori_loop(jnp.where(z == z_to, 1, 0), 8, one, 0)
 
     def await_all(ref, sem):
         some = ref.at[pl.ds(0, n_str - 1)]
         pltpu.make_async_copy(some, some, sem).wait()
 
-    for t in range(1, 4):
-        unit(t, t - 1, False)
-    send_a[...] = pack(0, 384)
-    pl.semaphore_wait(barrier, n_str - 1 + n_ib - 1)
-    send_all(send_a, recv_a, 0)
-    unit(0, 3, True)
-    send_b[...] = pack(384, 256)
-    send_all(send_b, recv_b, 1)
-
-    for load in loads[8:]:
-        load.wait()
-    recv_a[me] = send_a[me]
-    recv_b[me] = send_b[me]
+    chunk_a(0)
+    pl.semaphore_wait(barrier, 63 + n_ib - 1)
+    send(0, 0)
+    send(0, 1)
+    send(0, 2)
+    send(0, 3)
+    chunk_a(1)
+    send(0, 7)
+    send(0, 4)
+    send(0, 6)
+    send(0, 5)
+    chunk_b(0)
+    send(1, 0)
+    send(1, 1)
+    send(1, 2)
+    send(1, 3)
+    chunk_b(1)
+    send(1, 7)
+    send(1, 4)
+    send(1, 6)
+    send(1, 5)
+    mine = (z // 4) * 32 + y * 8 + (z % 4) * 2 + core
+    recv_a[me] = send_a[mine]
+    recv_b[me] = send_b[mine]
+    r = iota((512, 512), 0)
+    c = iota((512, 512), 1)
     from_cols = jnp.where(
         r == (c // 4 % 2) * 256 + (c // 8) * 4 + c % 4, 1.0, 0.0
     ).astype(BF16)
+    for load in loads[8:]:
+        load.wait()
     alpha = jnp.dot(a_ref[...], from_cols, preferred_element_type=F32).astype(BF16)
     eye = jnp.where(iota((256, 256), 0) == iota((256, 256), 1), 1.0, 0.0).astype(BF16)
     same = jnp.concatenate([as_ref[...], eye], axis=1)
@@ -195,19 +245,26 @@
 
     await_all(recv_a, str_recv.at[0])
     partial = jnp.dot(alpha, received(recv_a), preferred_element_type=F32).astype(BF16)
-    copies = []
     for u in range(3):
         part_s[u] = partial[:, u * 128 : (u + 1) * 128]
-        copy = pltpu.make_async_remote_copy(
+
+    def to_ib(u, ib_to):
+        return pltpu.make_async_remote_copy(
             src_ref=part_s.at[u],
             dst_ref=part_r.at[u],
             send_sem=ib_send.at[u],
             recv_sem=ib_recv.at[u],
-            device_id=(me, lax.rem(ib + 1 + u, n_ib)),
+            device_id=(me, ib_to),
             device_id_type=MESH,
         )
-        copy.start()
-        copies.append(copy)
+
+    for ib_to in range(n_ib):
+
+        @pl.when(ib_to != ib)
+        def _():
+            to_ib(lax.rem(ib_to - ib + n_ib - 1, n_ib), ib_to).start()
+
+    copies = [to_ib(u, lax.rem(ib + 1 + u, n_ib)) for u in range(3)]
     await_all(recv_b, str_recv.at[1])
     x = received(recv_b)
     total = jnp.dot(alpha, x[:, 0:128], preferred_element_type=F32) + jnp.dot(
@@ -253,8 +310,9 @@
             pltpu.VMEM((1024, 384), BF16),
             pltpu.VMEM((256, 512), BF16),
             pltpu.VMEM((256, 256), BF16),
-            pltpu.VMEM((256, 1024), BF16),
-            pltpu.VMEM((512, 640), BF16),
+            pltpu.VMEM((256, 256), BF16),
+            pltpu.VMEM((384, 1024), BF16),
+            pltpu.VMEM((256, 384), BF16),
             pltpu.VMEM((64, 8, 384), BF16),
             pltpu.VMEM((64, 8, 256), BF16),
             pltpu.VMEM((64, 8, 384), BF16),
@@ -266,6 +324,9 @@
             pltpu.SemaphoreType.DMA((2,)),
             pltpu.SemaphoreType.DMA((3,)),
             pltpu.SemaphoreType.DMA((3,)),
+            pltpu.SemaphoreType.REGULAR,
+            pltpu.SemaphoreType.REGULAR,
+            pltpu.SemaphoreType.REGULAR,
         ],
         compiler_params=pltpu.CompilerParams(
             collective_id=0, has_side_effects=True, vmem_limit_bytes=62 * 1024 * 1024

time: 31.8 us -> 30.2 us (0.950)
  the two profiles are of different devices: /device:TPU:1 before, /device:TPU:64 now
where the time goes in v3:
time: 30.2 us; the launch traced here: 30.1 us
  Pallas kernels  28.6 us (95%)
  local copies, waits for them, and re-layouts  1.47 us (5%)
    pallas_call x1, Pallas kernels, local(): pl.pallas_call(functools.partial(kernel, n_str, n_ib), out_shape=jax.Shap...  28.6 us
    unnamed x1, local copies, waits for them, and re-layouts  1.47 us

profile of v3, /device:TPU:64, one launch (start us, length us, event | category | flops | bytes accessed | tf_op | source)
XLA Modules:
  0.0 30.1 jit_solution(6318894910922531870)
XLA Ops:
  0.0 28.6 %shard_map.91 = bf16[256,128]{1,0:T(8,128)(2,1)} custom-call(bf16[256,4,128]{2,1,0:T(4,128)(2,1)} %bitcast.10, s32[1,256]{1,0:T(1,128)} %bitcast.14, s32[8,256]{1,0:T(8,128)} %bitcast.12, s32[8,256]{1,0:T(8,128)} %bitcast.13, s32[1,256]{1,0:T(1,128)} %bitcast.15, bf16[256,256]{1,0:T(8,128)(2,1)} %as_hbm.1, bf16[2,256,256]{2,1,0:T(8,128)(2,1)} %am_hbm.1, ...), custom_call_target="tpu_custom_call" | custom-call | tf_op jit(solution)/shard_map/pallas_call | solution.py:297
  28.6 1.5 %copy.11 = bf16[256,128]{1,0:T(8,128)(2,1)} copy(bf16[256,128]{1,0:T(8,128)(2,1)} %shard_map.91) | data formatting | bytes 131072

commit v4 on v3

--- a/solution.py
+++ b/solution.py
@@ -185,19 +185,23 @@
         src, dst = sends[which]
 
         def one(k, carry):
-            y_to, core_to = (y + k // 2) % 4, (core + k) % 2
+            y_to, core_to = k // 2, (core + k) % 2
             to = place(y_to, z_to, core_to)
-            pltpu.make_async_remote_copy(
-                src_ref=src.at[(z_to // 4) * 32 + y_to * 8 + (z_to % 4) * 2 + core_to],
-                dst_ref=dst.at[me],
-                send_sem=str_send.at[which],
-                recv_sem=str_recv.at[which],
-                device_id=(to, ib),
-                device_id_type=MESH,
-            ).start()
+
+            @pl.when(to != me)
+            def _():
+                pltpu.make_async_remote_copy(
+                    src_ref=src.at[(z_to // 4) * 32 + y_to * 8 + (z_to % 4) * 2 + core_to],
+                    dst_ref=dst.at[me],
+                    send_sem=str_send.at[which],
+                    recv_sem=str_recv.at[which],
+                    device_id=(to, ib),
+                    device_id_type=MESH,
+                ).start()
+
             return carry
 
-        lax.fori_loop(jnp.where(z == z_to, 1, 0), 8, one, 0)
+        lax.fori_loop(0, 8, one, 0)
 
     def await_all(ref, sem):
         some = ref.at[pl.ds(0, n_str - 1)]

time: 30.2 us -> 29.4 us (0.974)
  Pallas kernels: 28.6 us -> 27.8 us
    pallas_call x1, Pallas kernels: 28.6 us -> 27.8 us  [local(): pl.pallas_call(functools.partial(kernel, n_str, n_ib), out_shape=jax.Shap...]
where the time goes in v4:
time: 29.4 us; the launch traced here: 29.3 us
  Pallas kernels  27.8 us (95%)
  local copies, waits for them, and re-layouts  1.47 us (5%)
    pallas_call x1, Pallas kernels, local(): pl.pallas_call(functools.partial(kernel, n_str, n_ib), out_shape=jax.Shap...  27.8 us
    unnamed x1, local copies, waits for them, and re-layouts  1.47 us

profile of v4, /device:TPU:64, one launch (start us, length us, event | category | flops | bytes accessed | tf_op | source)
XLA Modules:
  0.0 29.3 jit_solution(8254768348332294298)
XLA Ops:
  0.0 27.8 %shard_map.91 = bf16[256,128]{1,0:T(8,128)(2,1)} custom-call(bf16[256,4,128]{2,1,0:T(4,128)(2,1)} %bitcast.10, s32[1,256]{1,0:T(1,128)} %bitcast.14, s32[8,256]{1,0:T(8,128)} %bitcast.12, s32[8,256]{1,0:T(8,128)} %bitcast.13, s32[1,256]{1,0:T(1,128)} %bitcast.15, bf16[256,256]{1,0:T(8,128)(2,1)} %as_hbm.1, bf16[2,256,256]{2,1,0:T(8,128)(2,1)} %am_hbm.1, ...), custom_call_target="tpu_custom_call" | custom-call | tf_op jit(solution)/shard_map/pallas_call | solution.py:301
  27.8 1.5 %copy.11 = bf16[256,128]{1,0:T(8,128)(2,1)} copy(bf16[256,128]{1,0:T(8,128)(2,1)} %shard_map.91) | data formatting | bytes 131072

commit v5 on v4

--- a/solution.py
+++ b/solution.py
@@ -300,7 +300,7 @@
     hbm = pl.BlockSpec(memory_space=pltpu.HBM)
     return pl.pallas_call(
         functools.partial(kernel, n_str, n_ib),
-        out_shape=jax.ShapeDtypeStruct((256, 128), BF16),
+        out_shape=pltpu.VMEM((256, 128), BF16),
         in_specs=[hbm] * 9,
         out_specs=pl.BlockSpec(memory_space=pltpu.VMEM),
         scratch_shapes=[

time: 29.4 us -> 27.9 us (0.949)
  local copies, waits for them, and re-layouts: 1.47 us -> 0.63 us
  Pallas kernels: 27.8 us -> 27.2 us
    unnamed x1, local copies, waits for them, and re-layouts: 1.47 us -> 0.63 us
    pallas_call x1, Pallas kernels: 27.8 us -> 27.2 us  [local(): pl.pallas_call(functools.partial(kernel, n_str, n_ib), out_shape=pltpu.VM...]
where the time goes in v5:
time: 27.9 us; the launch traced here: 27.8 us
  Pallas kernels  27.2 us (97%)
  local copies, waits for them, and re-layouts  0.63 us (2%)
    pallas_call x1, Pallas kernels, local(): pl.pallas_call(functools.partial(kernel, n_str, n_ib), out_shape=pltpu.VM...  27.2 us
    unnamed x1, local copies, waits for them, and re-layouts  0.63 us

profile of v5, /device:TPU:64, one launch (start us, length us, event | category | flops | bytes accessed | tf_op | source)
XLA Modules:
  0.0 27.8 jit_solution(4509949177459021144)
XLA Ops:
  0.0 27.2 %shard_map.91 = bf16[256,128]{1,0:T(8,128)(2,1)S(1)} custom-call(bf16[256,4,128]{2,1,0:T(4,128)(2,1)} %bitcast.10, s32[1,256]{1,0:T(1,128)} %bitcast.14, s32[8,256]{1,0:T(8,128)} %bitcast.12, s32[8,256]{1,0:T(8,128)} %bitcast.13, s32[1,256]{1,0:T(1,128)} %bitcast.15, bf16[256,256]{1,0:T(8,128)(2,1)} %as_hbm.1, bf16[2,256,256]{2,1,0:T(8,128)(2,1)} %am_hbm.1, ...), custom_call_target="tpu_custom_call" | custom-call | tf_op jit(solution)/shard_map/pallas_call | solution.py:301
  27.2 0.6 %copy.11 = bf16[256,128]{1,0:T(8,128)(2,1)} copy(bf16[256,128]{1,0:T(8,128)(2,1)S(1)} %shard_map.91) | data formatting | bytes 131072

commit v6 on v5

--- a/solution.py
+++ b/solution.py
@@ -10,6 +10,8 @@
 MESH = pl.DeviceIdType.MESH
 F32 = jnp.float32
 BF16 = jnp.bfloat16
+NEAR = (0, 1, 2, 3)
+FAR = (7, 4, 6, 5)
 
 
 def iota(shape, dim):
@@ -40,11 +42,15 @@
     a_ref,
     as_ref,
     msg_ref,
+    alpha_ref,
+    same_ref,
     g_ref,
     z_ref,
     send_a,
+    send_c,
     send_b,
     recv_a,
+    recv_c,
     recv_b,
     part_s,
     part_r,
@@ -128,17 +134,18 @@
     for load in loads[5:8]:
         load.wait()
 
-    def choose(t, half):
+    peers = [jnp.where(ib > u, u, u + 1) for u in range(3)]
+
+    def choose(position, half):
         owner = (sub // 8) * 16 + (4 * half + sub // 2 % 4) * 2 + sub % 2
-        position = lax.rem(ib + t, n_ib)
         owned = jnp.sum(
             jnp.where(lane == 4 * owner + position, order_f, 0.0), axis=1, keepdims=True
         )
         return jnp.where(lane_f == owned, 1.0, 0.0)
 
-    def units(ts, half, cols):
-        n = len(ts)
-        pick = jnp.concatenate([choose(t, half) for t in ts], axis=0)
+    def units(positions, half, cols):
+        n = len(positions)
+        pick = jnp.concatenate([choose(at, half) for at in positions], axis=0)
         irr_row = jnp.sum(pick * irr_f, axis=1, keepdims=True).astype(jnp.int32)
         pick = pick.astype(BF16)
         near = lax.dot_general(
@@ -168,18 +175,20 @@
         return rows.reshape(32, 8, width).astype(BF16)
 
     def chunk_a(half):
-        units((1, 2, 3), half, 256)
-        send_a[half * 32 : (half + 1) * 32] = pack(384)
+        units(peers, half, 256)
+        rows = pack(384)
+        send_a[half * 32 : (half + 1) * 32] = rows[:, :, :128]
+        send_c[half * 32 : (half + 1) * 32] = rows[:, :, 128:]
 
     def chunk_b(half):
-        pick, mixed = units((0,), half, 384)
+        pick, mixed = units([ib], half, 384)
         own = jnp.dot(pick, c_ref[...], preferred_element_type=F32).astype(BF16)
         for a in range(4):
             z_ref[a * 32 : (a + 1) * 32, 128:256] = own[:, a * 128 : (a + 1) * 128]
         z_ref[128:256, 128:256] = mixed[:, 256:384]
         send_b[half * 32 : (half + 1) * 32] = pack(256)
 
-    sends = ((send_a, recv_a), (send_b, recv_b))
+    sends = ((send_a, recv_a), (send_c, recv_c), (send_b, recv_b))
 
     def send(which, z_to):
         src, dst = sends[which]
@@ -209,27 +218,49 @@
 
     chunk_a(0)
     pl.semaphore_wait(barrier, 63 + n_ib - 1)
-    send(0, 0)
-    send(0, 1)
-    send(0, 2)
-    send(0, 3)
+    for z_to in NEAR:
+        send(0, z_to)
     chunk_a(1)
-    send(0, 7)
-    send(0, 4)
-    send(0, 6)
-    send(0, 5)
+    for z_to in FAR:
+        send(0, z_to)
+    for z_to in NEAR:
+        send(1, z_to)
     chunk_b(0)
-    send(1, 0)
-    send(1, 1)
-    send(1, 2)
-    send(1, 3)
+    for z_to in FAR[:2]:
+        send(1, z_to)
     chunk_b(1)
-    send(1, 7)
-    send(1, 4)
-    send(1, 6)
-    send(1, 5)
+    for z_to in FAR[2:]:
+        send(1, z_to)
+    for z_to in NEAR:
+        send(2, z_to)
+    for z_to in (4, 5, 6, 7):
+        send(2, z_to)
+
     mine = (z // 4) * 32 + y * 8 + (z % 4) * 2 + core
     recv_a[me] = send_a[mine]
+    recv_c[me] = send_c[mine]
+    def received(ref):
+        x = ref[...].astype(F32)
+        return x.reshape(512, x.shape[2]).astype(BF16)
+
+    def to_peer(u):
+        slot = jnp.where(ib < peers[u], ib, ib - 1)
+        return pltpu.make_async_remote_copy(
+            src_ref=part_s.at[u],
+            dst_ref=part_r.at[slot],
+            send_sem=ib_send.at[u],
+            recv_sem=ib_recv.at[slot],
+            device_id=(me, peers[u]),
+            device_id_type=MESH,
+        )
+
+    def first_peer():
+        await_all(recv_a, str_recv.at[0])
+        part_s[0] = jnp.dot(
+            alpha_ref[...], received(recv_a), preferred_element_type=F32
+        ).astype(BF16)
+        to_peer(0).start()
+
     recv_b[me] = send_b[mine]
     r = iota((512, 512), 0)
     c = iota((512, 512), 1)
@@ -238,50 +269,31 @@
     ).astype(BF16)
     for load in loads[8:]:
         load.wait()
-    alpha = jnp.dot(a_ref[...], from_cols, preferred_element_type=F32).astype(BF16)
+    alpha_ref[...] = jnp.dot(a_ref[...], from_cols, preferred_element_type=F32).astype(BF16)
     eye = jnp.where(iota((256, 256), 0) == iota((256, 256), 1), 1.0, 0.0).astype(BF16)
     same = jnp.concatenate([as_ref[...], eye], axis=1)
-    same = jnp.dot(same, from_cols, preferred_element_type=F32).astype(BF16)
-
-    def received(ref):
-        x = ref[...].astype(F32)
-        return x.reshape(512, x.shape[2]).astype(BF16)
-
-    await_all(recv_a, str_recv.at[0])
-    partial = jnp.dot(alpha, received(recv_a), preferred_element_type=F32).astype(BF16)
-    for u in range(3):
-        part_s[u] = partial[:, u * 128 : (u + 1) * 128]
-
-    def to_ib(u, ib_to):
-        return pltpu.make_async_remote_copy(
-            src_ref=part_s.at[u],
-            dst_ref=part_r.at[u],
-            send_sem=ib_send.at[u],
-            recv_sem=ib_recv.at[u],
-            device_id=(me, ib_to),
-            device_id_type=MESH,
-        )
-
-    for ib_to in range(n_ib):
-
-        @pl.when(ib_to != ib)
-        def _():
-            to_ib(lax.rem(ib_to - ib + n_ib - 1, n_ib), ib_to).start()
-
-    copies = [to_ib(u, lax.rem(ib + 1 + u, n_ib)) for u in range(3)]
-    await_all(recv_b, str_recv.at[1])
+    same_ref[...] = jnp.dot(same, from_cols, preferred_element_type=F32).astype(BF16)
+
+    first_peer()
+    await_all(recv_c, str_recv.at[1])
+    partial = jnp.dot(alpha_ref[...], received(recv_c), preferred_element_type=F32).astype(BF16)
+    for u in (1, 2):
+        part_s[u] = partial[:, (u - 1) * 128 : u * 128]
+        to_peer(u).start()
+    await_all(recv_b, str_recv.at[2])
     x = received(recv_b)
-    total = jnp.dot(alpha, x[:, 0:128], preferred_element_type=F32) + jnp.dot(
-        same, x[:, 128:256], preferred_element_type=F32
+    total = jnp.dot(alpha_ref[...], x[:, 0:128], preferred_element_type=F32) + jnp.dot(
+        same_ref[...], x[:, 128:256], preferred_element_type=F32
     )
-    for u in range(3):
-        copies[u].wait_recv()
-        total = total + part_r[u].astype(F32)
+    for k in range(3):
+        pltpu.make_async_copy(part_r.at[k], part_r.at[k], ib_recv.at[k]).wait()
+        total = total + part_r[k].astype(F32)
     out_ref[...] = total.astype(BF16)
     for u in range(3):
-        copies[u].wait_send()
+        to_peer(u).wait_send()
     await_all(send_a, str_send.at[0])
-    await_all(send_b, str_send.at[1])
+    await_all(send_c, str_send.at[1])
+    await_all(send_b, str_send.at[2])
 
 
 def local(
@@ -315,17 +327,21 @@
             pltpu.VMEM((256, 512), BF16),
             pltpu.VMEM((256, 256), BF16),
             pltpu.VMEM((256, 256), BF16),
+            pltpu.VMEM((256, 512), BF16),
+            pltpu.VMEM((256, 512), BF16),
             pltpu.VMEM((384, 1024), BF16),
             pltpu.VMEM((256, 384), BF16),
-            pltpu.VMEM((64, 8, 384), BF16),
+            pltpu.VMEM((64, 8, 128), BF16),
             pltpu.VMEM((64, 8, 256), BF16),
-            pltpu.VMEM((64, 8, 384), BF16),
+            pltpu.VMEM((64, 8, 256), BF16),
+            pltpu.VMEM((64, 8, 128), BF16),
+            pltpu.VMEM((64, 8, 256), BF16),
             pltpu.VMEM((64, 8, 256), BF16),
             pltpu.VMEM((3, 256, 128), BF16),
             pltpu.VMEM((3, 256, 128), BF16),
             pltpu.SemaphoreType.DMA((11,)),
-            pltpu.SemaphoreType.DMA((2,)),
-            pltpu.SemaphoreType.DMA((2,)),
+            pltpu.SemaphoreType.DMA((3,)),
+            pltpu.SemaphoreType.DMA((3,)),
             pltpu.SemaphoreType.DMA((3,)),
             pltpu.SemaphoreType.DMA((3,)),
             pltpu.SemaphoreType.REGULAR,

time: 27.9 us -> 27.5 us (0.986)
  the two profiles are of different devices: /device:TPU:64 before, /device:TPU:4 now
where the time goes in v6:
time: 27.5 us; the launch traced here: 27.4 us
  Pallas kernels  26.8 us (97%)
  local copies, waits for them, and re-layouts  0.63 us (2%)
    pallas_call x1, Pallas kernels, local(): pl.pallas_call(functools.partial(kernel, n_str, n_ib), out_shape=pltpu.VM...  26.8 us
    unnamed x1, local copies, waits for them, and re-layouts  0.63 us

profile of v6, /device:TPU:4, one launch (start us, length us, event | category | flops | bytes accessed | tf_op | source)
XLA Modules:
  0.0 27.4 jit_solution(17074907278273095741)
XLA Ops:
  0.0 26.8 %shard_map.91 = bf16[256,128]{1,0:T(8,128)(2,1)S(1)} custom-call(bf16[256,4,128]{2,1,0:T(4,128)(2,1)} %bitcast.10, s32[1,256]{1,0:T(1,128)} %bitcast.14, s32[8,256]{1,0:T(8,128)} %bitcast.12, s32[8,256]{1,0:T(8,128)} %bitcast.13, s32[1,256]{1,0:T(1,128)} %bitcast.15, bf16[256,256]{1,0:T(8,128)(2,1)} %as_hbm.1, bf16[2,256,256]{2,1,0:T(8,128)(2,1)} %am_hbm.1, ...), custom_call_target="tpu_custom_call" | custom-call | tf_op jit(solution)/shard_map/pallas_call | solution.py:313
  26.8 0.6 %copy.11 = bf16[256,128]{1,0:T(8,128)(2,1)} copy(bf16[256,128]{1,0:T(8,128)(2,1)S(1)} %shard_map.91) | data formatting | bytes 131072

commit v7 on v6

--- a/solution.py
+++ b/solution.py
@@ -12,6 +12,7 @@
 BF16 = jnp.bfloat16
 NEAR = (0, 1, 2, 3)
 FAR = (7, 4, 6, 5)
+FAR_LAST = (4, 5, 6, 7)
 
 
 def iota(shape, dim):
@@ -83,17 +84,11 @@
         load.start()
 
     y, z, core = me // 16, (me // 2) % 8, me % 2
-    late = z >= 4
 
     def place(y_to, z_to, core_to):
         return (((y_to % 4) * 8) + (z_to % 8)) * 2 + core_to % 2
 
     barrier = pltpu.get_barrier_semaphore()
-
-    def say(sem, y_to, z_to, core_to):
-        pl.semaphore_signal(
-            sem, inc=1, device_id=(place(y_to, z_to, core_to), ib), device_id_type=MESH
-        )
 
     for k in range(1, n_ib):
         pl.semaphore_signal(
@@ -233,7 +228,7 @@
         send(1, z_to)
     for z_to in NEAR:
         send(2, z_to)
-    for z_to in (4, 5, 6, 7):
+    for z_to in FAR_LAST:
         send(2, z_to)
 
     mine = (z // 4) * 32 + y * 8 + (z % 4) * 2 + core

time: 27.5 us -> 27.5 us (level)
  no operation moved by 1% of the time
where the time goes in v7:
time: 27.5 us; the launch traced here: 27.4 us
  Pallas kernels  26.8 us (97%)
  local copies, waits for them, and re-layouts  0.63 us (2%)
    pallas_call x1, Pallas kernels, local(): pl.pallas_call(functools.partial(kernel, n_str, n_ib), out_shape=pltpu.VM...  26.8 us
    unnamed x1, local copies, waits for them, and re-layouts  0.63 us

profile of v7, /device:TPU:4, one launch (start us, length us, event | category | flops | bytes accessed | tf_op | source)
XLA Modules:
  0.0 27.4 jit_solution(17074907278273095741)
XLA Ops:
  0.0 26.8 %shard_map.91 = bf16[256,128]{1,0:T(8,128)(2,1)S(1)} custom-call(bf16[256,4,128]{2,1,0:T(4,128)(2,1)} %bitcast.10, s32[1,256]{1,0:T(1,128)} %bitcast.14, s32[8,256]{1,0:T(8,128)} %bitcast.12, s32[8,256]{1,0:T(8,128)} %bitcast.13, s32[1,256]{1,0:T(1,128)} %bitcast.15, bf16[256,256]{1,0:T(8,128)(2,1)} %as_hbm.1, bf16[2,256,256]{2,1,0:T(8,128)(2,1)} %am_hbm.1, ...), custom_call_target="tpu_custom_call" | custom-call | tf_op jit(solution)/shard_map/pallas_call | solution.py:308
  26.8 0.6 %copy.11 = bf16[256,128]{1,0:T(8,128)(2,1)} copy(bf16[256,128]{1,0:T(8,128)(2,1)S(1)} %shard_map.91) | data formatting | bytes 131072

commit v8 on v7

--- a/solution.py
+++ b/solution.py
@@ -11,8 +11,9 @@
 F32 = jnp.float32
 BF16 = jnp.bfloat16
 NEAR = (0, 1, 2, 3)
-FAR = (7, 4, 6, 5)
-FAR_LAST = (4, 5, 6, 7)
+FAR = (4, 7, 5, 6)
+NEAR_LAST = ((0, 0), (0, 1), (1, 0), (0, 2), (1, 1), (0, 3), (2, 0), (1, 2), (2, 1), (1, 3), (3, 0), (2, 2), (3, 1), (2, 3), (3, 2), (3, 3))
+FAR_LAST = ((4, 0), (5, 0), (6, 0), (7, 0), (4, 1), (4, 2), (4, 3), (5, 1), (5, 2), (5, 3), (6, 1), (6, 2), (6, 3), (7, 1), (7, 2), (7, 3))
 
 
 def iota(shape, dim):
@@ -207,6 +208,24 @@
 
         lax.fori_loop(0, 8, one, 0)
 
+    def send_some(which, owners):
+        src, dst = sends[which]
+        for z_to, y_to in owners:
+            for k in range(2):
+                core_to = (core + k) % 2
+                to = place(y_to, z_to, core_to)
+
+                @pl.when(to != me)
+                def _():
+                    pltpu.make_async_remote_copy(
+                        src_ref=src.at[(z_to // 4) * 32 + y_to * 8 + (z_to % 4) * 2 + core_to],
+                        dst_ref=dst.at[me],
+                        send_sem=str_send.at[which],
+                        recv_sem=str_recv.at[which],
+                        device_id=(to, ib),
+                        device_id_type=MESH,
+                    ).start()
+
     def await_all(ref, sem):
         some = ref.at[pl.ds(0, n_str - 1)]
         pltpu.make_async_copy(some, some, sem).wait()
@@ -226,17 +245,14 @@
     chunk_b(1)
     for z_to in FAR[2:]:
         send(1, z_to)
-    for z_to in NEAR:
-        send(2, z_to)
-    for z_to in FAR_LAST:
-        send(2, z_to)
+    send_some(2, NEAR_LAST)
+    send_some(2, FAR_LAST)
 
     mine = (z // 4) * 32 + y * 8 + (z % 4) * 2 + core
     recv_a[me] = send_a[mine]
     recv_c[me] = send_c[mine]
     def received(ref):
-        x = ref[...].astype(F32)
-        return x.reshape(512, x.shape[2]).astype(BF16)
+        return ref[...].reshape(512, ref.shape[2])
 
     def to_peer(u):
         slot = jnp.where(ib < peers[u], ib, ib - 1)

time: 27.5 us -> 27.5 us (level)
  no operation moved by 1% of the time
where the time goes in v8:
time: 27.5 us; the launch traced here: 27.4 us
  Pallas kernels  26.8 us (97%)
  local copies, waits for them, and re-layouts  0.63 us (2%)
    pallas_call x1, Pallas kernels, local(): pl.pallas_call(functools.partial(kernel, n_str, n_ib), out_shape=pltpu.VM...  26.8 us
    unnamed x1, local copies, waits for them, and re-layouts  0.63 us

profile of v8, /device:TPU:4, one launch (start us, length us, event | category | flops | bytes accessed | tf_op | source)
XLA Modules:
  0.0 27.4 jit_solution(5175273436155807834)
XLA Ops:
  0.0 26.8 %shard_map.91 = bf16[256,128]{1,0:T(8,128)(2,1)S(1)} custom-call(bf16[256,4,128]{2,1,0:T(4,128)(2,1)} %bitcast.10, s32[1,256]{1,0:T(1,128)} %bitcast.14, s32[8,256]{1,0:T(8,128)} %bitcast.12, s32[8,256]{1,0:T(8,128)} %bitcast.13, s32[1,256]{1,0:T(1,128)} %bitcast.15, bf16[256,256]{1,0:T(8,128)(2,1)} %as_hbm.1, bf16[2,256,256]{2,1,0:T(8,128)(2,1)} %am_hbm.1, ...), custom_call_target="tpu_custom_call" | custom-call | tf_op jit(solution)/shard_map/pallas_call | solution.py:324
  26.8 0.6 %copy.11 = bf16[256,128]{1,0:T(8,128)(2,1)} copy(bf16[256,128]{1,0:T(8,128)(2,1)S(1)} %shard_map.91) | data formatting | bytes 131072

commit v9 on v8

--- a/solution.py
+++ b/solution.py
@@ -10,9 +10,8 @@
 MESH = pl.DeviceIdType.MESH
 F32 = jnp.float32
 BF16 = jnp.bfloat16
-NEAR = (0, 1, 2, 3)
 FAR = (4, 7, 5, 6)
-NEAR_LAST = ((0, 0), (0, 1), (1, 0), (0, 2), (1, 1), (0, 3), (2, 0), (1, 2), (2, 1), (1, 3), (3, 0), (2, 2), (3, 1), (2, 3), (3, 2), (3, 3))
+NEAR = ((0, 0), (0, 1), (1, 0), (0, 2), (1, 1), (0, 3), (2, 0), (1, 2), (2, 1), (1, 3), (3, 0), (2, 2), (3, 1), (2, 3), (3, 2), (3, 3))
 FAR_LAST = ((4, 0), (5, 0), (6, 0), (7, 0), (4, 1), (4, 2), (4, 3), (5, 1), (5, 2), (5, 3), (6, 1), (6, 2), (6, 3), (7, 1), (7, 2), (7, 3))
 
 
@@ -232,20 +231,18 @@
 
     chunk_a(0)
     pl.semaphore_wait(barrier, 63 + n_ib - 1)
-    for z_to in NEAR:
-        send(0, z_to)
+    send_some(0, NEAR)
     chunk_a(1)
     for z_to in FAR:
         send(0, z_to)
-    for z_to in NEAR:
-        send(1, z_to)
+    send_some(1, NEAR)
     chunk_b(0)
     for z_to in FAR[:2]:
         send(1, z_to)
     chunk_b(1)
     for z_to in FAR[2:]:
         send(1, z_to)
-    send_some(2, NEAR_LAST)
+    send_some(2, NEAR)
     send_some(2, FAR_LAST)
 
     mine = (z // 4) * 32 + y * 8 + (z % 4) * 2 + core

time: 27.5 us -> 27.3 us (level)
  no operation moved by 1% of the time
where the time goes in v9:
time: 27.3 us; the launch traced here: 27.2 us
  Pallas kernels  26.6 us (97%)
  local copies, waits for them, and re-layouts  0.63 us (2%)
    pallas_call x1, Pallas kernels, local(): pl.pallas_call(functools.partial(kernel, n_str, n_ib), out_shape=pltpu.VM...  26.6 us
    unnamed x1, local copies, waits for them, and re-layouts  0.63 us

profile of v9, /device:TPU:4, one launch (start us, length us, event | category | flops | bytes accessed | tf_op | source)
XLA Modules:
  0.0 27.2 jit_solution(3498088043306720600)
XLA Ops:
  0.0 26.6 %shard_map.91 = bf16[256,128]{1,0:T(8,128)(2,1)S(1)} custom-call(bf16[256,4,128]{2,1,0:T(4,128)(2,1)} %bitcast.10, s32[1,256]{1,0:T(1,128)} %bitcast.14, s32[8,256]{1,0:T(8,128)} %bitcast.12, s32[8,256]{1,0:T(8,128)} %bitcast.13, s32[1,256]{1,0:T(1,128)} %bitcast.15, bf16[256,256]{1,0:T(8,128)(2,1)} %as_hbm.1, bf16[2,256,256]{2,1,0:T(8,128)(2,1)} %am_hbm.1, ...), custom_call_target="tpu_custom_call" | custom-call | tf_op jit(solution)/shard_map/pallas_call | solution.py:321
  26.6 0.6 %copy.11 = bf16[256,128]{1,0:T(8,128)(2,1)} copy(bf16[256,128]{1,0:T(8,128)(2,1)S(1)} %shard_map.91) | data formatting | bytes 131072
